TPU v7x, 32 devices: a whole 2x2x4 slice. The times are simulated.
32 devices in a mesh: seq: 8 (over z, x), head: 4 (over y, core).
Axes of the slice: x: 2, y: 2, z: 4, core: 2. Of those that a mesh axis runs over, the one named last changes fastest.
Arguments:
- inputs: bfloat16 [6144, 8192], P('seq', 'head'), may hold values from -6 to 6
- log_decay: float32 [128, 6144], P('head', 'seq'), may hold values from -3 to 0, as said below
- write_proj: bfloat16 [6144, 128], P('seq'), may hold values from -0.5 to 0.5
- read_proj: bfloat16 [6144, 128], P('seq'), may hold values from -0.5 to 0.5
- grad_out: bfloat16 [6144, 8192], P('seq', 'head'), may hold values from -0.75 to 0.75
Outputs:
- outputs: bfloat16 [6144, 8192], P('seq', 'head')
- grad_inputs: bfloat16 [6144, 8192], P('seq', 'head')
- grad_write: float32 [6144, 128], P(('seq', 'head'))
- grad_read: float32 [6144, 128], P(('seq', 'head'))
Inputs may be any that keep to these rules, and one draw needn't show every extreme that they name: log_decay is negative everywhere.
All inputs are finite; a program needn't handle non-finite values.
Results may differ from a plain program's by a relative error of at most 0.0032.
Values sent between devices are 32-bit elements; how exact they have to be, the bound alone decides.
A program may use at most 192 MiB of HBM per device.

v0:
```python
import functools

import jax
import jax.numpy as jnp
from jax import lax
from jax.experimental import pallas as pl
from jax.experimental.pallas import tpu as pltpu
from jax.sharding import PartitionSpec as P

CHUNK = 128
LANES = 128
PARTS = 2
LAG = 2
MESH = pl.DeviceIdType.MESH
F32 = jnp.float32
BF16 = jnp.bfloat16


def dot(a, b, dims):
    return lax.dot_general(a, b, ((dims[0], dims[1]), ((), ())), preferred_element_type=F32)


def split(value):
    high = value.astype(BF16)
    return high, (value - high.astype(F32)).astype(BF16)


def kernel(
    sections, head_size,
    x_ref, g_ref, w_ref, r_ref, cum_ref,
    y_ref, dx_ref, grads_ref,
    decay_ref, y_acc, dx_acc, scores_ref, gscore_ref,
    local_s, local_g, in_s, in_g, out_s, out_g,
    send_s, recv_s, send_g, recv_g,
):
    tokens, width = x_ref.shape
    state = w_ref.shape[1]
    packs = width // LANES
    each = LANES // head_size
    chunks = tokens // CHUNK
    units = packs * PARTS
    part_rows = state // PARTS
    me = lax.axis_index("seq")
    back = sections - 1 - me
    has_prev = me > 0
    has_next = me < sections - 1

    barrier = pltpu.get_barrier_semaphore()

    @pl.when(has_prev)
    def _():
        pl.semaphore_signal(barrier, inc=1, device_id={"seq": me - 1}, device_id_type=MESH)

    @pl.when(has_next)
    def _():
        pl.semaphore_signal(barrier, inc=1, device_id={"seq": me + 1}, device_id_type=MESH)

    pl.semaphore_wait(barrier, has_prev.astype(jnp.int32) + has_next.astype(jnp.int32))

    def state_copy(unit):
        pack, rows = unit // PARTS, pl.ds((unit % PARTS) * part_rows, part_rows)
        return pltpu.make_async_remote_copy(
            src_ref=out_s.at[pack, rows],
            dst_ref=in_s.at[pack, rows],
            send_sem=send_s.at[unit],
            recv_sem=recv_s.at[unit],
            device_id={"seq": me + 1},
            device_id_type=MESH,
        )

    def grad_copy(unit):
        pack, rows = unit // PARTS, pl.ds((unit % PARTS) * part_rows, part_rows)
        return pltpu.make_async_remote_copy(
            src_ref=out_g.at[pack, rows],
            dst_ref=in_g.at[pack, rows],
            send_sem=send_g.at[unit],
            recv_sem=recv_g.at[unit],
            device_id={"seq": me - 1},
            device_id_type=MESH,
        )

    @pl.when(me == 0)
    def _():
        in_s[...] = jnp.zeros_like(in_s)

    @pl.when(back == 0)
    def _():
        in_g[...] = jnp.zeros_like(in_g)

    grads_ref[...] = jnp.zeros_like(grads_ref)
    gscore_ref[...] = jnp.zeros_like(gscore_ref)
    for k in range(chunks):
        rows = slice(k * CHUNK, (k + 1) * CHUNK)
        scores_ref[k] = dot(r_ref[rows, :], w_ref[rows, :], ((1,), (1,)))

    lane_head = lax.broadcasted_iota(jnp.int32, (CHUNK, LANES), 1) // head_size
    causal = lax.broadcasted_iota(jnp.int32, (CHUNK, CHUNK), 0) >= lax.broadcasted_iota(
        jnp.int32, (CHUNK, CHUNK), 1
    )

    def only(value, head):
        return jnp.where(lane_head == head, value, jnp.zeros_like(value))

    def local(pack):
        lanes = pl.ds(pl.multiple_of(pack * LANES, LANES), LANES)
        before = jnp.zeros((1, LANES), F32)
        carried = jnp.zeros((state, LANES), F32)
        tails, scaled_x, scaled_g, lasts = [], [], [], []
        for k in range(chunks):
            rows = slice(k * CHUNK, (k + 1) * CHUNK)
            cum_rows = cum_ref[pack, :, rows]
            spread = jnp.concatenate(
                [jnp.broadcast_to(cum_rows[h : h + 1], (head_size, CHUNK)) for h in range(each)], axis=0
            )
            decay = spread.T
            decay_ref[rows, lanes] = decay
            last = decay[CHUNK - 1 : CHUNK]
            lead = jnp.exp(decay - before)
            tail = jnp.exp(last - decay)
            x = x_ref[rows, lanes]
            g = g_ref[rows, lanes]
            x_tail = (x.astype(F32) * tail).astype(BF16)
            g_lead = (g.astype(F32) * lead).astype(BF16)
            x_heads = jnp.concatenate([only(x, h) for h in range(each)], axis=0)
            g_heads = jnp.concatenate([only(g, h) for h in range(each)], axis=0)
            product = dot(g, x_heads, ((1,), (1,)))
            mixes, gained = [], gscore_ref[k]
            for h in range(each):
                column = decay[:, h * head_size : h * head_size + 1]
                matrix = jnp.exp(jnp.where(causal, column - cum_rows[h : h + 1], -jnp.inf))
                mixes.append((scores_ref[k] * matrix).astype(BF16))
                gained = gained + product[:, h * CHUNK : (h + 1) * CHUNK] * matrix
            gscore_ref[k] = gained
            y = dot(jnp.concatenate(mixes, axis=1), x_heads, ((1,), (0,)))
            dx = dot(jnp.concatenate(mixes, axis=0), g_heads, ((0,), (0,)))
            dx_acc[rows, lanes] = dx
            if k:
                high, low = split(carried)
                r = r_ref[rows, :]
                y = y + lead * dot(
                    jnp.concatenate([r, r], axis=1), jnp.concatenate([high, low], axis=0), ((1,), (0,))
                )
                grads_ref[rows, state:] += dot(g_lead, high, ((1,), (1,)))
            y_acc[rows, lanes] = y
            carried = jnp.exp(last - before) * carried + dot(w_ref[rows, :], x_tail, ((0,), (0,)))
            lasts.append(jnp.exp(last - before))
            tails.append(tail)
            scaled_x.append(x_tail)
            scaled_g.append(g_lead)
            before = last
        local_s[pack] = carried
        carried = jnp.zeros((state, LANES), F32)
        for k in reversed(range(chunks)):
            rows = slice(k * CHUNK, (k + 1) * CHUNK)
            if k < chunks - 1:
                high, low = split(carried)
                w = w_ref[rows, :]
                dx_acc[rows, lanes] += tails[k] * dot(
                    jnp.concatenate([w, w], axis=1), jnp.concatenate([high, low], axis=0), ((1,), (0,))
                )
                grads_ref[rows, :state] += dot(scaled_x[k], high, ((1,), (1,)))
            carried = lasts[k] * carried + dot(r_ref[rows, :], scaled_g[k], ((0,), (0,)))
        local_g[pack] = carried

    def finish_state(pack):
        lanes = pl.ds(pl.multiple_of(pack * LANES, LANES), LANES)
        high, low = split(in_s[pack])
        both = jnp.concatenate([high, low], axis=0)
        for k in range(chunks):
            rows = slice(k * CHUNK, (k + 1) * CHUNK)
            r = r_ref[rows, :]
            lead = jnp.exp(decay_ref[rows, lanes])
            carried = dot(jnp.concatenate([r, r], axis=1), both, ((1,), (0,)))
            y_ref[rows, lanes] = (y_acc[rows, lanes] + lead * carried).astype(y_ref.dtype)
            g_lead = (g_ref[rows, lanes].astype(F32) * lead).astype(BF16)
            grads_ref[rows, state:] += dot(g_lead, high, ((1,), (1,)))

    def finish_grad(pack):
        lanes = pl.ds(pl.multiple_of(pack * LANES, LANES), LANES)
        high, low = split(in_g[pack])
        both = jnp.concatenate([high, low], axis=0)
        last = decay_ref[tokens - 1 : tokens, lanes]
        for k in range(chunks):
            rows = slice(k * CHUNK, (k + 1) * CHUNK)
            w = w_ref[rows, :]
            tail = jnp.exp(last - decay_ref[rows, lanes])
            carried = dot(jnp.concatenate([w, w], axis=1), both, ((1,), (0,)))
            dx_ref[rows, lanes] = (dx_acc[rows, lanes] + tail * carried).astype(dx_ref.dtype)
            x_tail = (x_ref[rows, lanes].astype(F32) * tail).astype(BF16)
            grads_ref[rows, :state] += dot(x_tail, high, ((1,), (1,)))

    def step(turn, nothing):
        @pl.when(jnp.logical_and(turn % PARTS == 0, turn < units))
        def _():
            local(turn // PARTS)

        unit_s = turn - LAG * me
        unit_g = turn - LAG * back

        def live(unit):
            return jnp.logical_and(unit >= 0, unit < units)

        def pass_on(unit, has_source, has_target, copy, held, local_ref, out_ref):
            pack, rows = unit // PARTS, pl.ds((unit % PARTS) * part_rows, part_rows)
            lanes = pl.ds(pl.multiple_of(pack * LANES, LANES), LANES)

            @pl.when(has_source)
            def _():
                copy(unit).wait_recv()

            @pl.when(has_target)
            def _():
                total = jnp.exp(decay_ref[tokens - 1 : tokens, lanes])
                out_ref[pack, rows] = total * held[pack, rows] + local_ref[pack, rows]
                copy(unit).start()

        @pl.when(live(unit_s))
        def _():
            pass_on(unit_s, has_prev, has_next, state_copy, in_s, local_s, out_s)

        @pl.when(live(unit_g))
        def _():
            pass_on(unit_g, has_next, has_prev, grad_copy, in_g, local_g, out_g)

        @pl.when(jnp.logical_and(live(unit_s), unit_s % PARTS == PARTS - 1))
        def _():
            finish_state(unit_s // PARTS)

        @pl.when(jnp.logical_and(live(unit_g), unit_g % PARTS == PARTS - 1))
        def _():
            finish_grad(unit_g // PARTS)

        return nothing

    lax.fori_loop(0, units + LAG * (sections - 1), step, 0)

    for k in range(chunks):
        rows = slice(k * CHUNK, (k + 1) * CHUNK)
        high, low = split(gscore_ref[k])
        r = r_ref[rows, :]
        w = w_ref[rows, :]
        grads_ref[rows, :state] += dot(
            jnp.concatenate([high, low], axis=0), jnp.concatenate([r, r], axis=0), ((0,), (0,))
        )
        grads_ref[rows, state:] += dot(
            jnp.concatenate([high, low], axis=1), jnp.concatenate([w, w], axis=0), ((1,), (0,))
        )

    def drain(unit, nothing):
        @pl.when(has_next)
        def _():
            state_copy(unit).wait_send()

        @pl.when(has_prev)
        def _():
            grad_copy(unit).wait_send()

        return nothing

    lax.fori_loop(0, units, drain, 0)


def per_device(inputs, log_decay, write_proj, read_proj, grad_out):
    tokens, width = inputs.shape
    heads = log_decay.shape[0]
    state = write_proj.shape[1]
    sections = lax.axis_size("seq")
    head_size = width // heads
    packs = width // LANES
    chunks = tokens // CHUNK
    units = packs * PARTS
    cumulative = jnp.cumsum(log_decay, axis=1).reshape(packs, LANES // head_size, tokens)
    vmem = pl.BlockSpec(memory_space=pltpu.VMEM)
    block = pltpu.VMEM((packs, state, LANES), F32)
    outputs, grad_inputs, grads = pl.pallas_call(
        functools.partial(kernel, sections, head_size),
        out_shape=(
            jax.ShapeDtypeStruct((tokens, width), BF16),
            jax.ShapeDtypeStruct((tokens, width), BF16),
            jax.ShapeDtypeStruct((tokens, 2 * state), F32),
        ),
        in_specs=[vmem] * 5,
        out_specs=(vmem, vmem, vmem),
        scratch_shapes=[
            pltpu.VMEM((tokens, width), F32),
            pltpu.VMEM((tokens, width), F32),
            pltpu.VMEM((tokens, width), F32),
            pltpu.VMEM((chunks, CHUNK, CHUNK), F32),
            pltpu.VMEM((chunks, CHUNK, CHUNK), F32),
            block, block, block, block, block, block,
            pltpu.SemaphoreType.DMA((units,)),
            pltpu.SemaphoreType.DMA((units,)),
            pltpu.SemaphoreType.DMA((units,)),
            pltpu.SemaphoreType.DMA((units,)),
        ],
        compiler_params=pltpu.CompilerParams(
            collective_id=0, has_side_effects=True, vmem_limit_bytes=56 * 1024 * 1024
        ),
    )(inputs, grad_out, write_proj, read_proj, cumulative)
    summed = lax.psum_scatter(grads, "head", scatter_dimension=0, tiled=True)
    return outputs, grad_inputs, summed[:, :state], summed[:, state:]


def solution(mesh):
    return jax.shard_map(
        per_device,
        mesh=mesh,
        in_specs=(
            P("seq", "head"),
            P("head", "seq"),
            P("seq", None),
            P("seq", None),
            P("seq", "head"),
        ),
        out_specs=(
            P("seq", "head"),
            P("seq", "head"),
            P(("seq", "head"), None),
            P(("seq", "head"), None),
        ),
        check_vma=False,
    )
```

profile of v0, /device:TPU:1, one launch (start us, length us, event | category | flops | bytes accessed | tf_op | source)
XLA Modules:
  0.0 140.4 jit_solution(6141170636937207991)
XLA Ops:
  7.2 0.0 copy-start
  7.2 0.0 reduce-scatter.2.cloned.1.call-start
  7.2 0.8 copy-done
  8.1 1.7 %reduce-window.6 = f32[32,6,128]{2,0,1:T(8,128)S(1)} reduce-window(f32[32,6,128]{2,0,1:T(8,128)S(1)} %copy_bitcast_fusion, f32[]{:T(128)} %constant.3.clone.1), window={size=1x1x128 pad=0_0x0_0x127_0}, to_apply=%region_0.0 | reduce-window | flops 3121152 | bytes 196612 | tf_op jit(solution)/shard_map/reduce-window
  9.8 0.2 slice_reduce_fusion
  10.0 0.1 broadcast_add_fusion
  10.1 0.1 copy.12
  10.2 0.7 reduce_window_sum.16.cum_ref
  10.9 82.3 %shard_map.84 = (bf16[768,2048]{1,0:T(8,128)(2,1)}, bf16[768,2048]{1,0:T(8,128)(2,1)}, f32[768,256]{1,0:T(8,128)}) custom-call(bf16[768,2048]{1,0:T(8,128)(2,1)} %x_ref.1, bf16[768,2048]{1,0:T(8,128)(2,1)} %g_ref.1, bf16[768,128]{1,0:T(8,128)(2,1)} %w_ref.1, bf16[768,128]{1,0:T(8,128)(2,1)} %r_ref.1, f32[16,2,768]{2,1,0:T(2,128)} %reduce_window_sum.16.cum_ref), custom_call_target="tpu_custom_call" | custom-call | tf_op jit(solution)/shard_map/pallas_call | solution.py:275
  93.2 0.0 reduce-scatter.2.cloned.1.call-update
  93.3 32.9 %reduce-scatter.2.cloned.1.call-done = f32[192,256]{1,0:T(8,128)} async-done(((f32[768,256]{1,0:T(8,128)}), f32[192,256]{1,0:T(8,128)}) %reduce-scatter.2.cloned.1.call-update) | async-done | bytes 196624 | tf_op jit(solution)/shard_map/reduce_scatter | solution.py:300
  126.2 1.6 %fusion = (f32[192,128]{1,0:T(8,128)}, f32[192,128]{1,0:T(8,128)}) fusion(f32[192,256]{1,0:T(8,128)} %reduce-scatter.2.cloned.1.call-done), kind=kLoop, calls=%fused_computation.3 | loop fusion | bytes 393216 | tf_op jit(solution)/shard_map/slice | solution.py:301
  127.8 0.0 copy-start.1
  127.8 4.1 %copy.17 = bf16[768,2048]{1,0:T(8,128)(2,1)} copy(bf16[768,2048]{1,0:T(8,128)(2,1)} %get-tuple-element.16) | data formatting | bytes 6291456
  131.9 0.0 copy-done.1
  131.9 1.7 %copy.18 = bf16[768,2048]{1,0:T(8,128)(2,1)} copy(bf16[768,2048]{1,0:T(8,128)(2,1)S(1)} %copy-done.1) | data formatting | bytes 6291456
  (2 shorter events, 0.0 us)
Async XLA Ops:
  7.2 0.9 copy-start
  7.2 119.0 %reduce-scatter.2.cloned.1.call-start = ((), (), s32[]{:S(2)}) async-start(), calls=%async_computation.1 | async-start | bytes 983040 | tf_op jit(solution)/shard_map/reduce_scatter | solution.py:300
  127.8 4.1 %copy-start.1 = (bf16[768,2048]{1,0:T(8,128)(2,1)S(1)}, bf16[768,2048]{1,0:T(8,128)(2,1)}, u32[]{:S(2)}) copy-start(bf16[768,2048]{1,0:T(8,128)(2,1)} %get-tuple-element.17) | copy-start | bytes 9437188
Sparse Core Ops, SparseCore 0:
  93.4 32.7 reduce-scatter.1
where the time goes:
time: 141 us; the launch traced here: 140 us
  Pallas kernels  82.3 us (58%)
  waiting for transfers between devices  32.9 us (23%)
  between operations  14.1 us (10%)
  local copies, waits for them, and re-layouts  9.2 us (7%)
  other arithmetic  1.86 us (1%)
    pallas_call x1, Pallas kernels, per_device(): pl.pallas_call(functools.partial(kernel, sections, head_size), out_shape=...  82.3 us
    reduce_scatter x1, waiting for transfers between devices, per_device(): summed = lax.psum_scatter(grads, 'head', scatter_dimension=0, tiled=True)  32.9 us
    unnamed x6, local copies, waits for them, and re-layouts  6.63 us
  transfers between devices with their start and end apart: 1, of which 1 were waited for; matrix products, arithmetic and copies ran while one was open for 0% of the time, Pallas kernels for 0%

commit v1 on v0

--- a/solution.py
+++ b/solution.py
@@ -10,7 +10,7 @@
 CHUNK = 128
 LANES = 128
 PARTS = 2
-LAG = 2
+LAG = 3
 MESH = pl.DeviceIdType.MESH
 F32 = jnp.float32
 BF16 = jnp.bfloat16
@@ -25,13 +25,19 @@
     return high, (value - high.astype(F32)).astype(BF16)
 
 
+def twice(shared, high, low):
+    return dot(
+        jnp.concatenate([shared, shared], axis=0), jnp.concatenate([high, low], axis=0), ((0,), (0,))
+    )
+
+
 def kernel(
-    sections, head_size,
+    sections, group, head_size,
     x_ref, g_ref, w_ref, r_ref, cum_ref,
-    y_ref, dx_ref, grads_ref,
-    decay_ref, y_acc, dx_acc, scores_ref, gscore_ref,
+    y_ref, dx_ref, gw_ref, gr_ref,
+    grads_ref, landed_ref, decay_ref, y_acc, dx_acc, scores_ref, gscore_ref,
     local_s, local_g, in_s, in_g, out_s, out_g,
-    send_s, recv_s, send_g, recv_g,
+    send_s, recv_s, send_g, recv_g, send_h, recv_h,
 ):
     tokens, width = x_ref.shape
     state = w_ref.shape[1]
@@ -55,7 +61,14 @@
     def _():
         pl.semaphore_signal(barrier, inc=1, device_id={"seq": me + 1}, device_id_type=MESH)
 
-    pl.semaphore_wait(barrier, has_prev.astype(jnp.int32) + has_next.astype(jnp.int32))
+    mine = lax.axis_index("head")
+    for gap in range(1, group):
+        pl.semaphore_signal(
+            barrier, inc=1, device_id={"head": lax.rem(mine + gap, group)}, device_id_type=MESH
+        )
+    pl.semaphore_wait(
+        barrier, has_prev.astype(jnp.int32) + has_next.astype(jnp.int32) + (group - 1)
+    )
 
     def state_copy(unit):
         pack, rows = unit // PARTS, pl.ds((unit % PARTS) * part_rows, part_rows)
@@ -105,7 +118,7 @@
         lanes = pl.ds(pl.multiple_of(pack * LANES, LANES), LANES)
         before = jnp.zeros((1, LANES), F32)
         carried = jnp.zeros((state, LANES), F32)
-        tails, scaled_x, scaled_g, lasts = [], [], [], []
+        tails, scaled_x, scaled_g, rest_g, lasts = [], [], [], [], []
         for k in range(chunks):
             rows = slice(k * CHUNK, (k + 1) * CHUNK)
             cum_rows = cum_ref[pack, :, rows]
@@ -119,8 +132,8 @@
             tail = jnp.exp(last - decay)
             x = x_ref[rows, lanes]
             g = g_ref[rows, lanes]
-            x_tail = (x.astype(F32) * tail).astype(BF16)
-            g_lead = (g.astype(F32) * lead).astype(BF16)
+            x_tail, x_rest = split(x.astype(F32) * tail)
+            g_lead, g_rest = split(g.astype(F32) * lead)
             x_heads = jnp.concatenate([only(x, h) for h in range(each)], axis=0)
             g_heads = jnp.concatenate([only(g, h) for h in range(each)], axis=0)
             product = dot(g, x_heads, ((1,), (1,)))
@@ -142,11 +155,12 @@
                 )
                 grads_ref[rows, state:] += dot(g_lead, high, ((1,), (1,)))
             y_acc[rows, lanes] = y
-            carried = jnp.exp(last - before) * carried + dot(w_ref[rows, :], x_tail, ((0,), (0,)))
+            carried = jnp.exp(last - before) * carried + twice(w_ref[rows, :], x_tail, x_rest)
             lasts.append(jnp.exp(last - before))
             tails.append(tail)
             scaled_x.append(x_tail)
             scaled_g.append(g_lead)
+            rest_g.append(g_rest)
             before = last
         local_s[pack] = carried
         carried = jnp.zeros((state, LANES), F32)
@@ -159,7 +173,7 @@
                     jnp.concatenate([w, w], axis=1), jnp.concatenate([high, low], axis=0), ((1,), (0,))
                 )
                 grads_ref[rows, :state] += dot(scaled_x[k], high, ((1,), (1,)))
-            carried = lasts[k] * carried + dot(r_ref[rows, :], scaled_g[k], ((0,), (0,)))
+            carried = lasts[k] * carried + twice(r_ref[rows, :], scaled_g[k], rest_g[k])
         local_g[pack] = carried
 
     def finish_state(pack):
@@ -246,6 +260,22 @@
             jnp.concatenate([high, low], axis=1), jnp.concatenate([w, w], axis=0), ((1,), (0,))
         )
 
+    share = tokens // group
+
+    def share_copy(gap):
+        peer = lax.rem(mine + gap, group)
+        return pltpu.make_async_remote_copy(
+            src_ref=grads_ref.at[pl.ds(pl.multiple_of(peer * share, share), share)],
+            dst_ref=landed_ref.at[gap - 1],
+            send_sem=send_h.at[gap - 1],
+            recv_sem=recv_h.at[gap - 1],
+            device_id={"head": peer},
+            device_id_type=MESH,
+        )
+
+    for gap in range(1, group):
+        share_copy(gap).start()
+
     def drain(unit, nothing):
         @pl.when(has_next)
         def _():
@@ -258,6 +288,12 @@
         return nothing
 
     lax.fori_loop(0, units, drain, 0)
+    summed = grads_ref[pl.ds(pl.multiple_of(mine * share, share), share)]
+    for gap in range(1, group):
+        share_copy(gap).wait()
+        summed = summed + landed_ref[gap - 1]
+    gw_ref[...] = summed[:, :state]
+    gr_ref[...] = summed[:, state:]
 
 
 def per_device(inputs, log_decay, write_proj, read_proj, grad_out):
@@ -265,6 +301,7 @@
     heads = log_decay.shape[0]
     state = write_proj.shape[1]
     sections = lax.axis_size("seq")
+    group = lax.axis_size("head")
     head_size = width // heads
     packs = width // LANES
     chunks = tokens // CHUNK
@@ -272,16 +309,19 @@
     cumulative = jnp.cumsum(log_decay, axis=1).reshape(packs, LANES // head_size, tokens)
     vmem = pl.BlockSpec(memory_space=pltpu.VMEM)
     block = pltpu.VMEM((packs, state, LANES), F32)
-    outputs, grad_inputs, grads = pl.pallas_call(
-        functools.partial(kernel, sections, head_size),
+    return pl.pallas_call(
+        functools.partial(kernel, sections, group, head_size),
         out_shape=(
             jax.ShapeDtypeStruct((tokens, width), BF16),
             jax.ShapeDtypeStruct((tokens, width), BF16),
-            jax.ShapeDtypeStruct((tokens, 2 * state), F32),
+            jax.ShapeDtypeStruct((tokens // group, state), F32),
+            jax.ShapeDtypeStruct((tokens // group, state), F32),
         ),
         in_specs=[vmem] * 5,
-        out_specs=(vmem, vmem, vmem),
+        out_specs=(vmem,) * 4,
         scratch_shapes=[
+            pltpu.VMEM((tokens, 2 * state), F32),
+            pltpu.VMEM((group - 1, tokens // group, 2 * state), F32),
             pltpu.VMEM((tokens, width), F32),
             pltpu.VMEM((tokens, width), F32),
             pltpu.VMEM((tokens, width), F32),
@@ -292,13 +332,13 @@
             pltpu.SemaphoreType.DMA((units,)),
             pltpu.SemaphoreType.DMA((units,)),
             pltpu.SemaphoreType.DMA((units,)),
+            pltpu.SemaphoreType.DMA((group - 1,)),
+            pltpu.SemaphoreType.DMA((group - 1,)),
         ],
         compiler_params=pltpu.CompilerParams(
             collective_id=0, has_side_effects=True, vmem_limit_bytes=56 * 1024 * 1024
         ),
     )(inputs, grad_out, write_proj, read_proj, cumulative)
-    summed = lax.psum_scatter(grads, "head", scatter_dimension=0, tiled=True)
-    return outputs, grad_inputs, summed[:, :state], summed[:, state:]
 
 
 def solution(mesh):

time: 141 us -> 106 us (0.75)
  waiting for transfers between devices: 32.9 us -> 0 us
  between operations: 14.1 us -> 0.68 us
  Pallas kernels: 82.3 us -> 94.1 us
    reduce_scatter x1 -> x0, waiting for transfers between devices: 32.9 us -> none  [per_device(): summed = lax.psum_scatter(grads, 'head', scatter_dimension=0, tiled=True)]
    pallas_call x1, Pallas kernels: 82.3 us -> 94.1 us  [per_device(): pl.pallas_call(functools.partial(kernel, sections, group, head_size), out...]
    slice x2 -> x1, local copies, waits for them, and re-layouts: 1.8 us -> 0.17 us  [the longest x1 1.63 us: per_device(): return (outputs, grad_inputs, summed[:, :state], summed[:, state:])]
    unnamed x6 -> x12, local copies, waits for them, and re-layouts: 6.63 us -> 7.97 us
  transfers between devices with their start and end apart: 1 -> 0, of which waited for: 1 -> 0; matrix products, arithmetic and copies ran while one was open for 0% -> 0% of each run, Pallas kernels for 0% -> 0%
where the time goes in v1:
time: 106 us
  Pallas kernels  94.1 us (89%)
  local copies, waits for them, and re-layouts  8.91 us (8%)
  other arithmetic  1.86 us (2%)
    pallas_call x1, Pallas kernels, per_device(): pl.pallas_call(functools.partial(kernel, sections, group, head_size), out...  94.1 us
    unnamed x12, local copies, waits for them, and re-layouts  7.97 us

profile of v1, /device:TPU:1, one launch (start us, length us, event | category | flops | bytes accessed | tf_op | source)
XLA Modules:
  0.0 105.5 jit_solution(16099421437229629468)
XLA Ops:
  0.6 0.0 copy-start
  0.6 0.9 copy-done
  1.5 1.7 %reduce-window.6 = f32[32,6,128]{2,0,1:T(8,128)S(1)} reduce-window(f32[32,6,128]{2,0,1:T(8,128)S(1)} %copy_bitcast_fusion, f32[]{:T(128)} %constant.3.clone.1), window={size=1x1x128 pad=0_0x0_0x127_0}, to_apply=%region_0.0 | reduce-window | flops 3121152 | bytes 196612 | tf_op jit(solution)/shard_map/reduce-window
  3.3 0.2 slice_reduce_fusion
  3.5 0.1 broadcast_add_fusion
  3.6 0.1 copy.12
  3.7 0.7 reduce_window_sum.16.cum_ref
  4.4 94.1 %shard_map.84 = (bf16[768,2048]{1,0:T(8,128)(2,1)}, bf16[768,2048]{1,0:T(8,128)(2,1)}, f32[192,128]{1,0:T(8,128)}, f32[192,128]{1,0:T(8,128)}) custom-call(bf16[768,2048]{1,0:T(8,128)(2,1)} %x_ref.1, bf16[768,2048]{1,0:T(8,128)(2,1)} %g_ref.1, bf16[768,128]{1,0:T(8,128)(2,1)} %w_ref.1, bf16[768,128]{1,0:T(8,128)(2,1)} %r_ref.1, ...), custom_call_target="tpu_custom_call" | custom-call | tf_op jit(solution)/shard_map/pallas_call | solution.py:312
  98.5 0.0 copy-start.1
  98.5 4.1 %copy.19 = bf16[768,2048]{1,0:T(8,128)(2,1)} copy(bf16[768,2048]{1,0:T(8,128)(2,1)} %get-tuple-element.8) | data formatting | bytes 6291456
  102.6 0.0 copy-done.1
  102.6 0.0 copy-start.3
  102.6 0.0 copy-start.2
  102.6 1.7 %copy.20 = bf16[768,2048]{1,0:T(8,128)(2,1)} copy(bf16[768,2048]{1,0:T(8,128)(2,1)S(1)} %copy-done.1) | data formatting | bytes 6291456
  104.3 0.0 copy-done.3
  104.3 0.6 copy.21
  104.9 0.0 copy-done.2
  104.9 0.6 copy.22
  (2 shorter events, 0.0 us)
Async XLA Ops:
  0.6 0.9 copy-start
  98.5 4.1 %copy-start.1 = (bf16[768,2048]{1,0:T(8,128)(2,1)S(1)}, bf16[768,2048]{1,0:T(8,128)(2,1)}, u32[]{:S(2)}) copy-start(bf16[768,2048]{1,0:T(8,128)(2,1)} %get-tuple-element.9) | copy-start | bytes 9437188
  102.6 1.7 %copy-start.3 = (f32[192,128]{1,0:T(8,128)S(1)}, f32[192,128]{1,0:T(8,128)}, u32[]{:S(2)}) copy-start(f32[192,128]{1,0:T(8,128)} %get-tuple-element.10) | copy-start | bytes 294916
  102.6 2.3 %copy-start.2 = (f32[192,128]{1,0:T(8,128)S(1)}, f32[192,128]{1,0:T(8,128)}, u32[]{:S(2)}) copy-start(f32[192,128]{1,0:T(8,128)} %get-tuple-element.11) | copy-start | bytes 294916

commit v2 on v1

--- a/solution.py
+++ b/solution.py
@@ -244,21 +244,23 @@
         def _():
             finish_grad(unit_g // PARTS)
 
+        @pl.when(turn == units - 1)
+        def _():
+            for k in range(chunks):
+                rows = slice(k * CHUNK, (k + 1) * CHUNK)
+                high, low = split(gscore_ref[k])
+                r = r_ref[rows, :]
+                w = w_ref[rows, :]
+                grads_ref[rows, :state] += dot(
+                    jnp.concatenate([high, low], axis=0), jnp.concatenate([r, r], axis=0), ((0,), (0,))
+                )
+                grads_ref[rows, state:] += dot(
+                    jnp.concatenate([high, low], axis=1), jnp.concatenate([w, w], axis=0), ((1,), (0,))
+                )
+
         return nothing
 
     lax.fori_loop(0, units + LAG * (sections - 1), step, 0)
-
-    for k in range(chunks):
-        rows = slice(k * CHUNK, (k + 1) * CHUNK)
-        high, low = split(gscore_ref[k])
-        r = r_ref[rows, :]
-        w = w_ref[rows, :]
-        grads_ref[rows, :state] += dot(
-            jnp.concatenate([high, low], axis=0), jnp.concatenate([r, r], axis=0), ((0,), (0,))
-        )
-        grads_ref[rows, state:] += dot(
-            jnp.concatenate([high, low], axis=1), jnp.concatenate([w, w], axis=0), ((1,), (0,))
-        )
 
     share = tokens // group
 

time: 106 us -> 105 us (level)
  no operation moved by 1% of the time
where the time goes in v2:
time: 105 us
  Pallas kernels  93.6 us (89%)
  local copies, waits for them, and re-layouts  8.91 us (8%)
  other arithmetic  1.86 us (2%)
    pallas_call x1, Pallas kernels, per_device(): pl.pallas_call(functools.partial(kernel, sections, group, head_size), out...  93.6 us
    unnamed x12, local copies, waits for them, and re-layouts  7.97 us

profile of v2, /device:TPU:1, one launch (start us, length us, event | category | flops | bytes accessed | tf_op | source)
XLA Modules:
  0.0 105.1 jit_solution(2828394639495564487)
XLA Ops:
  0.6 0.0 copy-start
  0.6 0.9 copy-done
  1.5 1.7 %reduce-window.6 = f32[32,6,128]{2,0,1:T(8,128)S(1)} reduce-window(f32[32,6,128]{2,0,1:T(8,128)S(1)} %copy_bitcast_fusion, f32[]{:T(128)} %constant.3.clone.1), window={size=1x1x128 pad=0_0x0_0x127_0}, to_apply=%region_0.0 | reduce-window | flops 3121152 | bytes 196612 | tf_op jit(solution)/shard_map/reduce-window
  3.3 0.2 slice_reduce_fusion
  3.5 0.1 broadcast_add_fusion
  3.6 0.1 copy.12
  3.7 0.7 reduce_window_sum.16.cum_ref
  4.4 93.6 %shard_map.84 = (bf16[768,2048]{1,0:T(8,128)(2,1)}, bf16[768,2048]{1,0:T(8,128)(2,1)}, f32[192,128]{1,0:T(8,128)}, f32[192,128]{1,0:T(8,128)}) custom-call(bf16[768,2048]{1,0:T(8,128)(2,1)} %x_ref.1, bf16[768,2048]{1,0:T(8,128)(2,1)} %g_ref.1, bf16[768,128]{1,0:T(8,128)(2,1)} %w_ref.1, bf16[768,128]{1,0:T(8,128)(2,1)} %r_ref.1, ...), custom_call_target="tpu_custom_call" | custom-call | tf_op jit(solution)/shard_map/pallas_call | solution.py:314
  98.0 0.0 copy-start.1
  98.0 4.1 %copy.19 = bf16[768,2048]{1,0:T(8,128)(2,1)} copy(bf16[768,2048]{1,0:T(8,128)(2,1)} %get-tuple-element.8) | data formatting | bytes 6291456
  102.1 0.0 copy-done.1
  102.1 0.0 copy-start.3
  102.1 0.0 copy-start.2
  102.1 1.7 %copy.20 = bf16[768,2048]{1,0:T(8,128)(2,1)} copy(bf16[768,2048]{1,0:T(8,128)(2,1)S(1)} %copy-done.1) | data formatting | bytes 6291456
  103.8 0.0 copy-done.3
  103.8 0.6 copy.21
  104.4 0.0 copy-done.2
  104.4 0.6 copy.22
  (2 shorter events, 0.0 us)
Async XLA Ops:
  0.6 0.9 copy-start
  98.0 4.1 %copy-start.1 = (bf16[768,2048]{1,0:T(8,128)(2,1)S(1)}, bf16[768,2048]{1,0:T(8,128)(2,1)}, u32[]{:S(2)}) copy-start(bf16[768,2048]{1,0:T(8,128)(2,1)} %get-tuple-element.9) | copy-start | bytes 9437188
  102.1 1.7 %copy-start.3 = (f32[192,128]{1,0:T(8,128)S(1)}, f32[192,128]{1,0:T(8,128)}, u32[]{:S(2)}) copy-start(f32[192,128]{1,0:T(8,128)} %get-tuple-element.10) | copy-start | bytes 294916
  102.1 2.3 %copy-start.2 = (f32[192,128]{1,0:T(8,128)S(1)}, f32[192,128]{1,0:T(8,128)}, u32[]{:S(2)}) copy-start(f32[192,128]{1,0:T(8,128)} %get-tuple-element.11) | copy-start | bytes 294916
